TPU v7x, 32 devices: a whole 2x2x4 slice. The times are simulated.
32 devices in a mesh: groups: 2 (over x), tm: 16 (over z, y, core).
Axes of the slice: x: 2, y: 2, z: 4, core: 2. Of those that a mesh axis runs over, the one named last changes fastest.
Arguments:
- signal: bfloat16 [128, 32768], P('groups', 'tm'), parts along dimension 0, may hold values from -24 to 24
- warp_blocks: int32 [4, 256], P('groups'), parts along dimension 0, may hold values from 0 to 255, as said below
- taps: int32 [4, 128, 8], P('groups'), parts along dimension 0, may hold values from 0 to 255
- tap_weights: float32 [4, 128, 8], P('groups'), parts along dimension 0, may hold values from -2 to 2
- replica: float32 [16384], replicated, may hold values from -0.046875 to 0.046875
Outputs:
- ambiguity: bfloat16 [4, 64, 32768], P('groups', None, 'tm'), parts along dimension 0
There are 2 independent parts, one for each index of `groups`. A program takes and returns all parts, laid end to end along the dimension named above; an argument that names none is the same for every part. Nothing has to cross between parts.
Inputs may be any that keep to these rules, and one draw needn't show every extreme that they name: warp_blocks[h, j] = ((e_h + 128 * j + floor(r_h * 128 * j / 32768)) // 128) mod 256, with floor division, for an integer epoch e_h in 0 to 32767 and an integer rate r_h with -983 <= r_h <= 983, both drawn for each hypothesis; hypothesis 0 has e_0 = 32640. Consecutive entries of one hypothesis therefore differ by 0, 1 or 2 modulo 256.
All inputs are finite; a program needn't handle non-finite values.
Results may differ from a plain program's by a relative error of at most 0.0062.
Values may be sent and summed in bfloat16 or wider, within the bound.
No kernel may reach another device: no remote copies, remote signals or barrier semaphores. Data moves between devices by JAX's collectives and lax.ppermute only.
A program may use at most 64 MiB of HBM per device.

v0:
```python
import functools

import jax
import jax.numpy as jnp
from jax import lax
from jax.experimental import pallas as pl
from jax.experimental.pallas import tpu as pltpu
from jax.sharding import PartitionSpec as P

BEAMS = 64
BLOCK = 128
PAIR = 2 * BLOCK
TAPS = 8
REPLICA = 16384
HYPS = 2
F32 = jnp.float32
BF16 = jnp.bfloat16

STRIPS = REPLICA // BLOCK + 2
STRIPS_PER_STEP = 10
TOEPLITZ_ROWS = STRIPS * BLOCK
NT = (((1,), (1,)), ((), ()))


def build_kernel(rev_ref, taps_ref, weights_ref, toeplitz_ref, interp_ref):
    step = pl.program_id(0)

    @pl.when(step == 0)
    def _():
        window = lax.broadcasted_iota(jnp.int32, (BLOCK, PAIR), 1)
        for hyp in range(HYPS):
            total = jnp.zeros((BLOCK, PAIR), F32)
            for tap in range(TAPS):
                hit = taps_ref[hyp, :, tap : tap + 1] == window
                total = total + jnp.where(hit, weights_ref[hyp, :, tap : tap + 1], 0.0)
            interp_ref[hyp * BLOCK : (hyp + 1) * BLOCK, :] = total.astype(BF16)

    previous = None
    for i in range(STRIPS_PER_STEP + 1):
        row = step * STRIPS_PER_STEP + i
        line = jnp.concatenate([rev_ref[pl.ds(row + 1, 1), :], rev_ref[pl.ds(row, 1), :]], axis=1)
        spread = jnp.broadcast_to(line, (BLOCK, PAIR))
        strip = pltpu.roll(spread, BLOCK, 1, stride=1, stride_axis=0)[:, :BLOCK].astype(BF16)
        if i > 0:
            rows = slice((i - 1) * BLOCK, i * BLOCK)
            toeplitz_ref[rows, :BLOCK] = strip
            toeplitz_ref[rows, BLOCK:] = previous
        previous = strip


def build(replica, taps, tap_weights):
    rev = jnp.pad(replica, (PAIR - 1, PAIR + 1)).reshape(-1, BLOCK)[:, ::-1]
    rows = STRIPS_PER_STEP * BLOCK
    return pl.pallas_call(
        build_kernel,
        grid=(STRIPS // STRIPS_PER_STEP,),
        out_shape=(
            jax.ShapeDtypeStruct((TOEPLITZ_ROWS, PAIR), BF16),
            jax.ShapeDtypeStruct((HYPS * BLOCK, PAIR), BF16),
        ),
        in_specs=[
            pl.BlockSpec(rev.shape, lambda g: (0, 0)),
            pl.BlockSpec(taps.shape, lambda g: (0, 0, 0)),
            pl.BlockSpec(tap_weights.shape, lambda g: (0, 0, 0)),
        ],
        out_specs=(
            pl.BlockSpec((rows, PAIR), lambda g: (g, 0)),
            pl.BlockSpec((HYPS * BLOCK, PAIR), lambda g: (0, 0)),
        ),
        cost_estimate=pl.CostEstimate(flops=10_000_000, bytes_accessed=16_000_000, transcendentals=0),
        name="build_toeplitz",
    )(rev, taps, tap_weights)


def split_sum(total):
    high = total.astype(BF16).astype(F32)
    middle = (total - high).astype(BF16).astype(F32)
    return high, middle, total - high - middle


def correlate_kernel(plan, sources_ref, source_ref, interp_ref, toeplitz_hbm, out_ref, wide_ref, acc_ref, toeplitz_ref, sems, *scratch):
    lines, wide, steps, segments = plan["lines"], plan["wide"], plan["steps"], plan["segments"]
    rows = acc_ref.shape[0]
    depth = wide * PAIR
    blocks = rows // lines

    def fetch(step):
        start = step * depth
        size = min(depth, TOEPLITZ_ROWS - start)
        part = pl.ds(start, size)
        return pltpu.make_async_copy(toeplitz_hbm.at[part, :], toeplitz_ref.at[part, :], sems.at[step])

    for step in range(steps):
        fetch(step).start()

    if plan["fused"]:
        next_ref, first_ref, second_ref, warped_ref = scratch
        beams = lines // HYPS
        chunk = 256

        def product(start, half):
            return lax.dot_general(
                source_ref[pl.ds(start, chunk), :],
                interp_ref[:, half * BLOCK : (half + 1) * BLOCK],
                NT,
                preferred_element_type=F32,
            )

        for start in range(0, rows, chunk):
            next_ref[start : start + chunk, :] = product(start, 1)
        next_ref[rows : rows + 8, :] = next_ref[0:8, :]
        for start in range(0, rows, chunk):
            value = product(start, 0) + next_ref[start + beams : start + beams + chunk, :]
            first_ref[start : start + chunk, :] = value[:, :BLOCK]
            second_ref[start + beams : start + beams + chunk, :] = value[:, BLOCK:]
        upper = lax.broadcasted_iota(jnp.int32, (lines, BLOCK), 0) < beams

        unroll = 8

        def gather(group, carry):
            for inner in range(unroll):
                block = group * unroll + inner
                for half in range(2):
                    at_first = sources_ref[0, 2 * block + half] * beams
                    at_second = sources_ref[1, 2 * block + half] * beams
                    value = jnp.where(
                        upper, first_ref[pl.ds(at_first, lines), :], second_ref[pl.ds(at_second, lines), :]
                    )
                    warped_ref[pl.ds(pl.multiple_of(block * lines, lines), lines), half * BLOCK : (half + 1) * BLOCK] = value
            return carry

        lax.fori_loop(0, blocks // unroll, gather, 0)
        extra = warped_ref.shape[0] - rows
        warped_ref[rows:, :] = warped_ref[:extra, :]
        piece = 256
        for start in range(0, wide_ref.shape[0], piece):
            for shift in range(wide):
                from_row = start + shift * lines
                wide_ref[start : start + piece, shift * PAIR : (shift + 1) * PAIR] = warped_ref[
                    from_row : from_row + piece, :
                ].astype(BF16)
    else:
        wide_ref[...] = source_ref[...]

    def step_product(step, offset):
        return jnp.dot(
            wide_ref[pl.ds(offset, rows), :],
            toeplitz_ref[pl.ds(step * depth, depth), :],
            preferred_element_type=F32,
        )

    fetch(0).wait()
    acc_ref[...] = step_product(0, 0)

    whole = TOEPLITZ_ROWS // depth
    for step in range(1, whole):
        fetch(step).wait()
        acc_ref[...] += step_product(step, step * wide * lines)
    if whole < steps:
        fetch(whole).wait()
        left = TOEPLITZ_ROWS - whole * depth
        acc_ref[...] += jnp.dot(
            wide_ref[whole * wide * lines : whole * wide * lines + rows, :left],
            toeplitz_ref[whole * depth :, :],
            preferred_element_type=F32,
        )

    share = rows // segments
    sums = jnp.zeros((8, PAIR), F32)
    for segment in range(segments):
        value = acc_ref[segment * share : (segment + 1) * share, :]
        power = value * value
        sums = sums + jnp.sum(power.reshape(share // 8, 8, PAIR), axis=0)
        out_ref[segment, :share, :] = power[:, :BLOCK].astype(BF16)
        out_ref[segment, share : 2 * share, :] = power[:, BLOCK:].astype(BF16)
    sums = jnp.sum(sums, axis=1, keepdims=True)
    line = lax.broadcasted_iota(jnp.int32, (8, 1), 0)
    is_first = line % lines < lines // HYPS
    place = lax.broadcasted_iota(jnp.int32, (16, BLOCK), 0)
    tail = jnp.zeros((16, BLOCK), F32)
    for hyp in range(HYPS):
        total = jnp.sum(jnp.where(is_first == (hyp == 0), sums, 0.0), axis=0, keepdims=True)
        for index, part in enumerate(split_sum(total)):
            tail = jnp.where(place == hyp * 3 + index, part, tail)
    tail = tail.astype(BF16)
    for segment in range(segments):
        out_ref[segment, 2 * share :, :] = tail


def correlate(plan, sources, source, interp, toeplitz):
    lines, wide, steps, segments, rows = (plan[k] for k in ("lines", "wide", "steps", "segments", "rows"))
    wide_rows = rows + REPLICA // PAIR * lines
    share = rows // segments
    scratch = [
        pltpu.VMEM((wide_rows, wide * PAIR), BF16),
        pltpu.VMEM((rows, PAIR), F32),
        pltpu.VMEM((TOEPLITZ_ROWS, PAIR), BF16),
        pltpu.SemaphoreType.DMA((steps,)),
    ]
    if plan["fused"]:
        scratch += [
            pltpu.VMEM((rows + 8, PAIR), F32),
            pltpu.VMEM((rows + 8, BLOCK), F32),
            pltpu.VMEM((rows + 8, BLOCK), F32),
            pltpu.VMEM((wide_rows + wide * lines, PAIR), F32),
        ]
    vmem = pl.BlockSpec(memory_space=pltpu.VMEM)
    return pl.pallas_call(
        functools.partial(correlate_kernel, plan),
        out_shape=jax.ShapeDtypeStruct((segments, 2 * share + 16, BLOCK), BF16),
        in_specs=[pl.BlockSpec(memory_space=pltpu.SMEM), vmem, vmem, pl.BlockSpec(memory_space=pl.ANY)],
        out_specs=vmem,
        scratch_shapes=scratch,
        compiler_params=pltpu.CompilerParams(vmem_limit_bytes=48 * 1024 * 1024),
        cost_estimate=pl.CostEstimate(
            flops=2 * rows * TOEPLITZ_ROWS * PAIR, bytes_accessed=12_000_000, transcendentals=0
        ),
        name="warp_correlate",
    )(sources, source, interp, toeplitz)


def levels_of(sums, count):
    return [jnp.sum(sums[:, 3 * hyp : 3 * hyp + 3, :1]) / count + 1e-06 for hyp in range(HYPS)]


def finish_kernel(count, power_ref, sums_ref, out_ref):
    sums = sums_ref[...].astype(F32)
    upper = lax.broadcasted_iota(jnp.int32, (8, BLOCK), 0) < 4
    place = lax.broadcasted_iota(jnp.int32, sums.shape, 1)
    inverse = []
    for hyp in range(HYPS):
        picked = jnp.where((place >= 3 * hyp) & (place < 3 * hyp + 3), sums, 0.0)
        total = jnp.sum(jnp.sum(picked, axis=0), axis=0, keepdims=True)
        inverse.append(1.0 / (total / count + 1e-06))
    scale = jnp.where(upper, inverse[0], inverse[1])
    for half in range(2):
        for pair in range(4):
            tiles = [
                power_ref[device, half * 64 + pair * 16 : half * 64 + pair * 16 + 16, :].astype(F32)
                for device in range(4)
            ]
            for inner in range(2):
                parts = [tile[inner * 8 : inner * 8 + 8, :] * scale for tile in tiles]
                turned = [pltpu.roll(part, 4, 0) for part in parts]
                lane = (pair * 2 + inner) * PAIR + half * BLOCK
                low = [jnp.where(upper, parts[d], turned[d + 1]) for d in (0, 2)]
                high = [jnp.where(upper, turned[d], parts[d + 1]) for d in (0, 2)]
                out_ref[0, :, lane : lane + BLOCK] = jnp.concatenate(low, axis=0).astype(BF16)
                out_ref[1, :, lane : lane + BLOCK] = jnp.concatenate(high, axis=0).astype(BF16)


def finish(received, count):
    segments = received.shape[0]
    return pl.pallas_call(
        functools.partial(finish_kernel, count),
        grid=(segments // 4,),
        out_shape=jax.ShapeDtypeStruct((HYPS, segments * 4, 8 * PAIR), BF16),
        in_specs=[
            pl.BlockSpec((4, 144, BLOCK), lambda g: (g, 0, 0)),
            pl.BlockSpec((segments, 16, BLOCK), lambda g: (0, 8, 0)),
        ],
        out_specs=pl.BlockSpec((HYPS, 16, 8 * PAIR), lambda g: (0, g, 0)),
        cost_estimate=pl.CostEstimate(flops=1_000_000, bytes_accessed=1_200_000, transcendentals=0),
        name="scale_power",
    )(received, received)


def finish_plain(received, count, lines):
    segments = received.shape[0]
    beams = lines // HYPS
    blocks = (received.shape[1] - 16) // (2 * lines)
    levels = jnp.stack(levels_of(received[:, -16:, :].astype(F32), count))
    power = received[:, :-16, :].reshape(segments, 2, blocks, HYPS, beams, BLOCK).astype(F32)
    scaled = (power / levels[:, None, None]).astype(BF16)
    return scaled.transpose(3, 0, 4, 2, 1, 5).reshape(HYPS, segments * beams, blocks * PAIR)


def widen(received, sources, interp, beams, wide, wide_blocks):
    blocks = received.reshape(-1, beams, BLOCK)
    windows = jnp.concatenate([blocks, jnp.roll(blocks, -1, axis=0)], axis=2)
    warped = lax.dot_general(
        windows, interp, (((2,), (1,)), ((), ())), preferred_element_type=F32
    ).astype(BF16)
    warped = warped.reshape(-1, beams, HYPS, BLOCK)
    chosen = jnp.stack([jnp.take(warped[:, :, hyp], sources[hyp], axis=0) for hyp in range(HYPS)], axis=1)
    count = chosen.shape[0] // 2
    pairs = chosen.reshape(count, 2, HYPS, beams, BLOCK).transpose(0, 2, 3, 1, 4)
    pairs = pairs.reshape(count, HYPS * beams, PAIR)
    index = jnp.arange(wide_blocks)
    spread = [jnp.take(pairs, (index + shift) % count, axis=0) for shift in range(wide)]
    return jnp.concatenate(spread, axis=2).reshape(wide_blocks * HYPS * beams, wide * PAIR)


def body(signal, warp_blocks, taps, tap_weights, replica):
    segments = lax.axis_size("tm")
    beams = signal.shape[0] // segments
    samples = signal.shape[1] * segments
    local = signal.shape[1] // BLOCK
    lines = HYPS * beams
    send = signal.reshape(segments, beams, local, BLOCK).transpose(0, 2, 1, 3)
    send = send.reshape(segments, local * beams, BLOCK)
    received = lax.all_to_all(send, "tm", split_axis=0, concat_axis=0, tiled=True)
    toeplitz, interp = build(replica, taps, tap_weights)
    wide = max(2, 16 // lines)
    plan = dict(
        lines=lines,
        wide=wide,
        steps=-(-TOEPLITZ_ROWS // (wide * PAIR)),
        segments=segments,
        rows=samples // PAIR * lines,
        fused=lines == 8,
    )
    if plan["fused"]:
        source = received.reshape(-1, BLOCK)
    else:
        source = widen(received, warp_blocks, interp, beams, wide, samples // PAIR + REPLICA // PAIR)
    sent = correlate(plan, warp_blocks, source, interp, toeplitz)
    back = lax.all_to_all(sent, "tm", split_axis=0, concat_axis=0, tiled=True)
    count = float(BEAMS * samples)
    if plan["fused"] and signal.shape[1] == 8 * PAIR:
        return finish(back, count)
    return finish_plain(back, count, lines)


def solution(mesh):
    in_specs = (
        P("groups", "tm"),
        P("groups", None),
        P("groups", None, None),
        P("groups", None, None),
        P(),
    )
    out_specs = P("groups", None, "tm")
    return jax.shard_map(body, mesh=mesh, in_specs=in_specs, out_specs=out_specs, check_vma=False)
```

profile of v0, /device:TPU:0, one launch (start us, length us, event | category | flops | bytes accessed | tf_op | source)
XLA Modules:
  0.0 72.9 jit_solution(14813082347881404493)
XLA Ops:
  0.0 1.0 %copy.9 = bf16[8,8,16,128]{3,2,1,0:T(8,128)(2,1)S(1)} copy(bf16[8,8,16,128]{3,1,2,0:T(8,128)(2,1)} %bitcast.11) | data formatting | bytes 524288
  1.0 0.8 %copy.6 = bf16[16,16,4,128]{3,2,1,0:T(4,128)(2,1)} copy(bf16[16,16,4,128]{3,1,2,0:T(8,128)(2,1)S(1)} %bitcast.10) | data formatting | bytes 524288 | tf_op jit(solution)/shard_map/transpose | solution.py:300
  1.8 7.4 %all-to-all-start = ((bf16[16,64,128]{2,1,0:T(8,128)(2,1)}), bf16[16,64,128]{2,1,0:T(8,128)(2,1)S(1)}, u32[]{:S(2)}, u32[]{:S(2)}) async-start(bf16[16,64,128]{2,1,0:T(8,128)(2,1)} %bitcast.1), calls=%async_computation | async-start | bytes 524288 | tf_op jit(solution)/shard_map/all_to_all | solution.py:302
  9.2 0.9 %pad_bitcast_fusion = f32[132,128]{1,0:T(8,128)S(1)} fusion(f32[16384]{0:T(1024)} %param.9), kind=kLoop, calls=%fused_computation | loop fusion | bytes 133120 | tf_op jit(solution)/shard_map/reshape | solution.py:52
  10.1 0.8 %rev.3.rev_ref = f32[132,128]{1,0:T(8,128)} reverse(f32[132,128]{1,0:T(8,128)S(1)} %pad_bitcast_fusion), dimensions={1} | reverse | bytes 135168 | tf_op jit(solution)/shard_map/rev | solution.py:52
  11.0 1.5 %copy.7.taps_ref = s32[2,128,8]{2,1,0:T(8,128)} copy(s32[2,128,8]{1,2,0:T(8,128)} %param.7) | data formatting | bytes 16384 | tf_op args[2]
  12.4 1.5 %copy.8.weights_ref = f32[2,128,8]{2,1,0:T(8,128)} copy(f32[2,128,8]{1,2,0:T(8,128)} %param.8) | data formatting | bytes 16384 | tf_op args[3]
  13.9 9.5 %build_toeplitz.1 = (bf16[16640,256]{1,0:T(8,128)(2,1)}, bf16[256,256]{1,0:T(8,128)(2,1)}) custom-call(f32[132,128]{1,0:T(8,128)} %rev.3.rev_ref, s32[2,128,8]{2,1,0:T(8,128)} %copy.7.taps_ref, f32[2,128,8]{2,1,0:T(8,128)} %copy.8.weights_ref), custom_call_target="tpu_custom_call" | custom-call | flops 10000000 | bytes 16000000 | tf_op jit(solution)/shard_map/build_toeplitz/pallas_call | solution.py:54
  23.4 0.0 all-to-all-done
  23.4 0.0 copy-start
  23.4 0.9 %copy-done = bf16[256,256]{1,0:T(8,128)(2,1)S(1)} copy-done((bf16[256,256]{1,0:T(8,128)(2,1)S(1)}, bf16[256,256]{1,0:T(8,128)(2,1)}, u32[]{:S(2)}) %copy-start) | copy-done | bytes 131096
  24.3 0.0 copy-start.1
  24.3 0.7 copy-done.1
  25.0 21.4 %warp_correlate.1 = bf16[16,144,128]{2,1,0:T(8,128)(2,1)S(1)} custom-call(s32[2,256]{1,0:T(2,128)S(1)} %copy-done.1, bf16[1024,128]{1,0:T(8,128)(2,1)S(1)} %bitcast.9, bf16[256,256]{1,0:T(8,128)(2,1)S(1)} %copy-done, bf16[16640,256]{1,0:T(8,128)(2,1)} %get-tuple-element.8.toeplitz_hbm), custom_call_target="tpu_custom_call" | custom-call | flops 8724152320 | bytes 12000000 | tf_op jit(solution)/shard_map/warp_correlate/pallas_call | solution.py:208
  46.4 23.2 %all_to_all.10.power_ref.sums_ref = bf16[16,144,128]{2,1,0:T(8,128)(2,1)} all-to-all(bf16[16,144,128]{2,1,0:T(8,128)(2,1)S(1)} %warp_correlate.1), channel_id=1, replica_groups=mesh['groups'=2,'tm'=16] {'tm'}, dimensions={0} | all-to-all | bytes 1179648 | tf_op jit(solution)/shard_map/all_to_all | solution.py:318
  69.6 3.3 %scale_power.1 = bf16[2,64,2048]{2,1,0:T(8,128)(2,1)} custom-call(bf16[16,144,128]{2,1,0:T(8,128)(2,1)} %all_to_all.10.power_ref.sums_ref, bf16[16,144,128]{2,1,0:T(8,128)(2,1)} %all_to_all.10.power_ref.sums_ref), custom_call_target="tpu_custom_call" | custom-call | flops 1000000 | bytes 1200000 | tf_op jit(solution)/shard_map/scale_power/pallas_call | solution.py:254
Async XLA Ops:
  1.8 21.6 %all-to-all-start = ((bf16[16,64,128]{2,1,0:T(8,128)(2,1)}), bf16[16,64,128]{2,1,0:T(8,128)(2,1)S(1)}, u32[]{:S(2)}, u32[]{:S(2)}) async-start(bf16[16,64,128]{2,1,0:T(8,128)(2,1)} %bitcast.1), calls=%async_computation | async-start | bytes 524288 | tf_op jit(solution)/shard_map/all_to_all | solution.py:302
  23.4 0.9 %copy-start = (bf16[256,256]{1,0:T(8,128)(2,1)S(1)}, bf16[256,256]{1,0:T(8,128)(2,1)}, u32[]{:S(2)}) copy-start(bf16[256,256]{1,0:T(8,128)(2,1)} %get-tuple-element.7.interp_ref) | copy-start | bytes 393220
  24.3 0.7 copy-start.1
where the time goes:
time: 73.4 us; the launch traced here: 72.9 us
  Pallas kernels  34.2 us (47%)
  blocking collectives  23.2 us (32%)
  local copies, waits for them, and re-layouts  8.11 us (11%)
  starting transfers between devices  7.39 us (10%)
    all_to_all x1, blocking collectives, body(): back = lax.all_to_all(sent, 'tm', split_axis=0, concat_axis=0, tiled=True)  23.2 us
    pallas_call x1, Pallas kernels, correlate(): pl.pallas_call(functools.partial(correlate_kernel, plan), out_shape=jax.S...  21.4 us
    pallas_call x1, Pallas kernels, build(): pl.pallas_call(build_kernel, grid=(STRIPS // STRIPS_PER_STEP,), out_shape...  9.49 us
    all_to_all x1, starting transfers between devices, body(): lax.all_to_all(send, 'tm', split_axis=0, concat_axis=0, tiled=True)  7.39 us
    unnamed x7, local copies, waits for them, and re-layouts  5.54 us
    pallas_call x1, Pallas kernels, finish(): pl.pallas_call(functools.partial(finish_kernel, count), grid=(segments //...  3.3 us
  transfers between devices with their start and end apart: 1, of which 0 were waited for; matrix products, arithmetic and copies ran while one was open for 6% of the time, Pallas kernels for 13%

commit v1 on v0

v1 whole, which is shorter than its diff:
```python
import functools

import jax
import jax.numpy as jnp
from jax import lax
from jax.experimental import pallas as pl
from jax.experimental.pallas import tpu as pltpu
from jax.sharding import PartitionSpec as P

BEAMS = 64
BLOCK = 128
PAIR = 2 * BLOCK
TAPS = 8
REPLICA = 16384
HYPS = 2
F32 = jnp.float32
BF16 = jnp.bfloat16

STRIPS = REPLICA // BLOCK + 2
STRIPS_PER_LOOP = 10
TOEPLITZ_ROWS = STRIPS * BLOCK
VMEM = pl.BlockSpec(memory_space=pltpu.VMEM)


def spread_kernel(signal_ref, out_ref):
    upper = lax.broadcasted_iota(jnp.int32, (8, BLOCK), 0) < 4
    groups, blocks = signal_ref.shape[0] // 16, signal_ref.shape[1] // BLOCK
    for group in range(groups):
        for quad in range(0, blocks, 4):
            tiles = []
            for block in range(quad, quad + 4):
                value = signal_ref[group * 16 : group * 16 + 16, block * BLOCK : (block + 1) * BLOCK].astype(F32)
                tiles.append((value[:8], value[8:]))
            for half in range(2):
                parts = [tile[half] for tile in tiles]
                turned = [pltpu.roll(part, 4, 0) for part in parts]
                first = [jnp.where(upper, parts[d], turned[d + 1]) for d in (0, 2)]
                second = [jnp.where(upper, turned[d], parts[d + 1]) for d in (0, 2)]
                device = group * 4 + half * 2
                rows = slice(quad * 4, quad * 4 + 16)
                out_ref[device, rows, :] = jnp.concatenate(first, axis=0).astype(BF16)
                out_ref[device + 1, rows, :] = jnp.concatenate(second, axis=0).astype(BF16)


def spread(signal, segments):
    beams, blocks = signal.shape[0] // segments, signal.shape[1] // BLOCK
    if beams != 4 or signal.shape[0] % 16 or blocks % 4:
        send = signal.reshape(segments, beams, blocks, BLOCK).transpose(0, 2, 1, 3)
        return send.reshape(segments, blocks * beams, BLOCK)
    return pl.pallas_call(
        spread_kernel,
        out_shape=jax.ShapeDtypeStruct((segments, blocks * beams, BLOCK), BF16),
        in_specs=[VMEM],
        out_specs=VMEM,
        name="spread_beams",
    )(signal)


def build_kernel(replica_ref, taps_ref, weights_ref, strips_ref, interp_ref, line_ref):
    window = lax.broadcasted_iota(jnp.int32, (PAIR, BLOCK), 0)
    for hyp in range(HYPS):
        total = jnp.zeros((PAIR, BLOCK), F32)
        for tap in range(TAPS):
            hit = taps_ref[hyp, tap : tap + 1, :] == window
            total = total + jnp.where(hit, weights_ref[hyp, tap : tap + 1, :], 0.0)
        interp_ref[:, hyp * BLOCK : (hyp + 1) * BLOCK] = total.astype(BF16)

    count = replica_ref.shape[0]
    row = lax.broadcasted_iota(jnp.int32, (BLOCK, BLOCK), 0)
    col = lax.broadcasted_iota(jnp.int32, (BLOCK, BLOCK), 1)
    keep = ((row == 0) & (col == 0)).astype(F32).astype(BF16)
    turn = ((row + col == BLOCK) & (col > 0)).astype(F32).astype(BF16)
    rounded = replica_ref[...].astype(BF16)
    line_ref[...] = jnp.zeros_like(line_ref)
    line_ref[1 : count + 1, :] = jnp.dot(rounded, keep, preferred_element_type=F32)
    line_ref[2 : count + 2, :] += jnp.dot(rounded, turn, preferred_element_type=F32)
    below = col >= row

    def rotations(index):
        line = jnp.broadcast_to(line_ref[pl.ds(index, 1), :], (BLOCK, BLOCK))
        return pltpu.roll(line, 0, 1, stride=1, stride_axis=0)

    def some(group, now):
        for inner in range(STRIPS_PER_LOOP):
            strip = group * STRIPS_PER_LOOP + inner
            after = rotations(strip + 1)
            rows = pl.ds(pl.multiple_of(strip * BLOCK, BLOCK), BLOCK)
            strips_ref[rows, :] = jnp.where(below, now, after).astype(BF16)
            now = after
        return now

    lax.fori_loop(0, STRIPS // STRIPS_PER_LOOP, some, rotations(0))
    strips_ref[STRIPS * BLOCK :, :] = jnp.zeros((BLOCK, BLOCK), BF16)


def build(replica, taps, tap_weights):
    return pl.pallas_call(
        build_kernel,
        out_shape=(
            jax.ShapeDtypeStruct((TOEPLITZ_ROWS + BLOCK, BLOCK), BF16),
            jax.ShapeDtypeStruct((PAIR, HYPS * BLOCK), BF16),
        ),
        in_specs=[VMEM] * 3,
        out_specs=(VMEM, VMEM),
        scratch_shapes=[pltpu.VMEM((STRIPS + 14, BLOCK), F32)],
        compiler_params=pltpu.CompilerParams(vmem_limit_bytes=16 * 1024 * 1024),
        cost_estimate=pl.CostEstimate(flops=10_000_000, bytes_accessed=16_000_000, transcendentals=0),
        name="build_toeplitz",
    )(replica.reshape(-1, BLOCK), taps.transpose(0, 2, 1), tap_weights.transpose(0, 2, 1))


def split_sum(total):
    high = total.astype(BF16).astype(F32)
    middle = (total - high).astype(BF16).astype(F32)
    return high, middle, total - high - middle


def warp_rows(sources_ref, source_ref, interp_ref, wide_ref, next_ref, warped_ref):
    rows = source_ref.shape[0]
    blocks = rows // 8
    upper = lax.broadcasted_iota(jnp.int32, (8, BLOCK), 0) < 4
    chunk = 256

    def product(start, half):
        return jnp.dot(
            source_ref[start : start + chunk, :],
            interp_ref[half * BLOCK : (half + 1) * BLOCK, :],
            preferred_element_type=F32,
        )

    for start in range(0, rows, chunk):
        next_ref[start : start + chunk, :] = product(start, 1)
    next_ref[rows : rows + 8, :] = next_ref[0:8, :]
    for start in range(0, rows, chunk):
        value = product(start, 0) + next_ref[start + 4 : start + 4 + chunk, :]
        first = value[:, :BLOCK].reshape(chunk // 8, 8, BLOCK)
        second = value[:, BLOCK:].reshape(chunk // 8, 8, BLOCK)
        even = jnp.where(upper, first, pltpu.roll(second, 4, 1))
        odd = jnp.where(upper, pltpu.roll(first, 4, 1), second)
        both = jnp.stack([even, odd], axis=1).reshape(2 * chunk, BLOCK)
        warped_ref[2 * start : 2 * start + 2 * chunk, :] = both

    def block_of(index):
        halves = []
        for half in range(2):
            picked = [
                warped_ref[pl.ds(pl.multiple_of(sources_ref[hyp, 2 * index + half] * 8, 8), 8), :]
                for hyp in range(HYPS)
            ]
            halves.append(jnp.where(upper, picked[0], picked[1]))
        return jnp.concatenate(halves, axis=1)

    unroll = 4

    def gather(group, before):
        for inner in range(unroll):
            pair = group * unroll + inner
            now, after = block_of(2 * pair), block_of(2 * pair + 1)
            place = pl.multiple_of(pair * 16, 16)
            wide_ref[pl.ds(place + 16, 16), :PAIR] = jnp.concatenate([now, after], axis=0).astype(BF16)
            wide_ref[pl.ds(place, 16), PAIR:] = jnp.concatenate([before, now], axis=0).astype(BF16)
            before = after
        return before

    last = lax.fori_loop(0, blocks // 2 // unroll, gather, jnp.zeros((8, PAIR), F32))
    wide_ref[rows : rows + 16, PAIR:] = jnp.concatenate([last, block_of(0)], axis=0).astype(BF16)
    extra = wide_ref.shape[0] - 16 - rows
    wide_ref[16 + rows :, :] = wide_ref[16 : 16 + extra, :]


def correlate_kernel(plan, sources_ref, source_ref, interp_ref, strips_ref, out_ref, wide_ref, acc_ref, *scratch):
    lines, wide, segments = plan["lines"], plan["wide"], plan["segments"]
    rows = acc_ref.shape[0]
    depth = wide * PAIR
    if plan["fused"]:
        warp_rows(sources_ref, source_ref, interp_ref, wide_ref, *scratch)
        base = 16
    else:
        wide_ref[...] = source_ref[...]
        base = 0

    parts = 2
    part = rows // parts
    share = rows // segments
    sums = jnp.zeros((8, PAIR), F32)
    for index in range(parts):
        for start in range(0, TOEPLITZ_ROWS, depth):
            size = min(depth, TOEPLITZ_ROWS - start)
            matrix = jnp.concatenate(
                [strips_ref[start + BLOCK : start + BLOCK + size, :], strips_ref[start : start + size, :]], axis=1
            )
            offset = base + index * part + start // PAIR * lines
            value = jnp.dot(wide_ref[offset : offset + part, :size], matrix, preferred_element_type=F32)
            if start == 0:
                acc_ref[index * part : (index + 1) * part, :] = value
            else:
                acc_ref[index * part : (index + 1) * part, :] += value
        for segment in range(index * segments // parts, (index + 1) * segments // parts):
            value = acc_ref[segment * share : (segment + 1) * share, :]
            power = value * value
            sums = sums + jnp.sum(power.reshape(share // 8, 8, PAIR), axis=0)
            out_ref[segment, :share, :] = power[:, :BLOCK].astype(BF16)
            out_ref[segment, share : 2 * share, :] = power[:, BLOCK:].astype(BF16)
    sums = jnp.sum(sums, axis=1, keepdims=True)
    line = lax.broadcasted_iota(jnp.int32, (8, 1), 0)
    is_first = line % lines < lines // HYPS
    place = lax.broadcasted_iota(jnp.int32, (16, BLOCK), 0)
    tail = jnp.zeros((16, BLOCK), F32)
    for hyp in range(HYPS):
        total = jnp.sum(jnp.where(is_first == (hyp == 0), sums, 0.0), axis=0, keepdims=True)
        for index, piece in enumerate(split_sum(total)):
            tail = jnp.where(place == hyp * 3 + index, piece, tail)
    tail = tail.astype(BF16)
    for segment in range(segments):
        out_ref[segment, 2 * share :, :] = tail


def correlate(plan, sources, source, interp, strips):
    lines, wide, segments, rows = (plan[k] for k in ("lines", "wide", "segments", "rows"))
    wide_rows = rows + REPLICA // PAIR * lines
    share = rows // segments
    scratch = [pltpu.VMEM((wide_rows + (16 if plan["fused"] else 0), wide * PAIR), BF16), pltpu.VMEM((rows, PAIR), F32)]
    if plan["fused"]:
        scratch += [pltpu.VMEM((rows + 8, PAIR), F32), pltpu.VMEM((2 * rows, BLOCK), F32)]
    return pl.pallas_call(
        functools.partial(correlate_kernel, plan),
        out_shape=jax.ShapeDtypeStruct((segments, 2 * share + 16, BLOCK), BF16),
        in_specs=[pl.BlockSpec(memory_space=pltpu.SMEM), VMEM, VMEM, VMEM],
        out_specs=VMEM,
        scratch_shapes=scratch,
        compiler_params=pltpu.CompilerParams(vmem_limit_bytes=24 * 1024 * 1024),
        cost_estimate=pl.CostEstimate(
            flops=2 * rows * TOEPLITZ_ROWS * PAIR, bytes_accessed=12_000_000, transcendentals=0
        ),
        name="warp_correlate",
    )(sources, source, interp, strips)


def levels_of(sums, count):
    return [jnp.sum(sums[:, 3 * hyp : 3 * hyp + 3, :1]) / count + 1e-06 for hyp in range(HYPS)]


def finish_kernel(count, power_ref, sums_ref, out_ref):
    sums = sums_ref[...].astype(F32)
    upper = lax.broadcasted_iota(jnp.int32, (8, BLOCK), 0) < 4
    place = lax.broadcasted_iota(jnp.int32, sums.shape, 1)
    inverse = []
    for hyp in range(HYPS):
        picked = jnp.where((place >= 3 * hyp) & (place < 3 * hyp + 3), sums, 0.0)
        total = jnp.sum(jnp.sum(picked, axis=0), axis=0, keepdims=True)
        inverse.append(1.0 / (total / count + 1e-06))
    scale = jnp.where(upper, inverse[0], inverse[1])
    for half in range(2):
        for pair in range(4):
            tiles = [
                power_ref[device, half * 64 + pair * 16 : half * 64 + pair * 16 + 16, :].astype(F32)
                for device in range(4)
            ]
            for inner in range(2):
                parts = [tile[inner * 8 : inner * 8 + 8, :] * scale for tile in tiles]
                turned = [pltpu.roll(part, 4, 0) for part in parts]
                lane = (pair * 2 + inner) * PAIR + half * BLOCK
                low = [jnp.where(upper, parts[d], turned[d + 1]) for d in (0, 2)]
                high = [jnp.where(upper, turned[d], parts[d + 1]) for d in (0, 2)]
                out_ref[0, :, lane : lane + BLOCK] = jnp.concatenate(low, axis=0).astype(BF16)
                out_ref[1, :, lane : lane + BLOCK] = jnp.concatenate(high, axis=0).astype(BF16)


def finish(received, count):
    segments = received.shape[0]
    return pl.pallas_call(
        functools.partial(finish_kernel, count),
        grid=(segments // 4,),
        out_shape=jax.ShapeDtypeStruct((HYPS, segments * 4, 8 * PAIR), BF16),
        in_specs=[
            pl.BlockSpec((4, 144, BLOCK), lambda g: (g, 0, 0)),
            pl.BlockSpec((segments, 16, BLOCK), lambda g: (0, 8, 0)),
        ],
        out_specs=pl.BlockSpec((HYPS, 16, 8 * PAIR), lambda g: (0, g, 0)),
        cost_estimate=pl.CostEstimate(flops=1_000_000, bytes_accessed=1_200_000, transcendentals=0),
        name="scale_power",
    )(received, received)


def finish_plain(received, count, lines):
    segments = received.shape[0]
    beams = lines // HYPS
    blocks = (received.shape[1] - 16) // (2 * lines)
    levels = jnp.stack(levels_of(received[:, -16:, :].astype(F32), count))
    power = received[:, :-16, :].reshape(segments, 2, blocks, HYPS, beams, BLOCK).astype(F32)
    scaled = (power / levels[:, None, None]).astype(BF16)
    return scaled.transpose(3, 0, 4, 2, 1, 5).reshape(HYPS, segments * beams, blocks * PAIR)


def widen(received, sources, interp, beams, wide, wide_blocks):
    blocks = received.reshape(-1, beams, BLOCK)
    windows = jnp.concatenate([blocks, jnp.roll(blocks, -1, axis=0)], axis=2)
    warped = lax.dot_general(
        windows, interp, (((2,), (0,)), ((), ())), preferred_element_type=F32
    ).astype(BF16)
    warped = warped.reshape(-1, beams, HYPS, BLOCK)
    chosen = jnp.stack([jnp.take(warped[:, :, hyp], sources[hyp], axis=0) for hyp in range(HYPS)], axis=1)
    count = chosen.shape[0] // 2
    pairs = chosen.reshape(count, 2, HYPS, beams, BLOCK).transpose(0, 2, 3, 1, 4)
    pairs = pairs.reshape(count, HYPS * beams, PAIR)
    index = jnp.arange(wide_blocks)
    spread = [jnp.take(pairs, (index + shift) % count, axis=0) for shift in range(wide)]
    return jnp.concatenate(spread, axis=2).reshape(wide_blocks * HYPS * beams, wide * PAIR)


def body(signal, warp_blocks, taps, tap_weights, replica):
    segments = lax.axis_size("tm")
    beams = signal.shape[0] // segments
    samples = signal.shape[1] * segments
    lines = HYPS * beams
    received = lax.all_to_all(spread(signal, segments), "tm", split_axis=0, concat_axis=0, tiled=True)
    strips, interp = build(replica, taps, tap_weights)
    wide = max(2, 16 // lines)
    plan = dict(
        lines=lines,
        wide=wide,
        segments=segments,
        rows=samples // PAIR * lines,
        fused=lines == 8,
    )
    if plan["fused"]:
        source = received.reshape(-1, BLOCK)
    else:
        source = widen(received, warp_blocks, interp, beams, wide, samples // PAIR + REPLICA // PAIR)
    sent = correlate(plan, warp_blocks, source, interp, strips)
    back = lax.all_to_all(sent, "tm", split_axis=0, concat_axis=0, tiled=True)
    count = float(BEAMS * samples)
    if plan["fused"] and signal.shape[1] == 8 * PAIR:
        return finish(back, count)
    return finish_plain(back, count, lines)


def solution(mesh):
    in_specs = (
        P("groups", "tm"),
        P("groups", None),
        P("groups", None, None),
        P("groups", None, None),
        P(),
    )
    out_specs = P("groups", None, "tm")
    return jax.shard_map(body, mesh=mesh, in_specs=in_specs, out_specs=out_specs, check_vma=False)
```

time: 73.4 us -> 57.7 us (0.79)
  Pallas kernels: 34.2 us -> 18.9 us
  waiting for transfers between devices: 0.01 us -> 3.21 us
  blocking collectives: 23.2 us -> 20.5 us
  local copies, waits for them, and re-layouts: 8.11 us -> 7.09 us
    pallas_call x1, Pallas kernels: 21.4 us -> 11.3 us  [correlate(): pl.pallas_call(functools.partial(correlate_kernel, plan), out_shape=jax.S...]
    pallas_call x1 -> x2, Pallas kernels: 9.49 us -> 4.33 us  [the longest x1 2.62 us: build(): pl.pallas_call(build_kernel, out_shape=(jax.ShapeDtypeStruct((TOEPLITZ_RO...]
    all_to_all x1, waiting for transfers between devices: 0.01 us -> 3.21 us  [body(): lax.all_to_all(spread(signal, segments), 'tm', split_axis=0, concat_axis=...]
    all_to_all x1, blocking collectives: 23.2 us -> 20.5 us  [body(): back = lax.all_to_all(sent, 'tm', split_axis=0, concat_axis=0, tiled=True)]
    unnamed x7 -> x12, local copies, waits for them, and re-layouts: 5.54 us -> 7.09 us
    reshape x1 -> x0, local copies, waits for them, and re-layouts: 0.92 us -> none  [build(): rev = jnp.pad(replica, (PAIR - 1, PAIR + 1)).reshape(-1, BLOCK)[:, ::-1]]
    rev x1 -> x0, local copies, waits for them, and re-layouts: 0.82 us -> none  [build(): rev = jnp.pad(replica, (PAIR - 1, PAIR + 1)).reshape(-1, BLOCK)[:, ::-1]]
    transpose x1 -> x0, local copies, waits for them, and re-layouts: 0.82 us -> none  [body(): send = signal.reshape(segments, beams, local, BLOCK).transpose(0, 2, 1, 3)]
  transfers between devices with their start and end apart: 1 -> 1, of which waited for: 0 -> 1; matrix products, arithmetic and copies ran while one was open for 6% -> 0% of each run, Pallas kernels for 13% -> 5%
where the time goes in v1:
time: 57.7 us; the launch traced here: 57.2 us
  blocking collectives  20.5 us (36%)
  Pallas kernels  18.9 us (33%)
  starting transfers between devices  7.39 us (13%)
  local copies, waits for them, and re-layouts  7.09 us (12%)
  waiting for transfers between devices  3.21 us (6%)
    all_to_all x1, blocking collectives, body(): back = lax.all_to_all(sent, 'tm', split_axis=0, concat_axis=0, tiled=True)  20.5 us
    pallas_call x1, Pallas kernels, correlate(): pl.pallas_call(functools.partial(correlate_kernel, plan), out_shape=jax.S...  11.3 us
    all_to_all x1, starting transfers between devices, body(): lax.all_to_all(spread(signal, segments), 'tm', split_axis=0, concat_axis=...  7.39 us
    unnamed x12, local copies, waits for them, and re-layouts  7.09 us
    pallas_call x1, Pallas kernels, finish(): pl.pallas_call(functools.partial(finish_kernel, count), grid=(segments //...  3.3 us
    all_to_all x1, waiting for transfers between devices, body(): lax.all_to_all(spread(signal, segments), 'tm', split_axis=0, concat_axis=...  3.21 us
    pallas_call x1, Pallas kernels, build(): pl.pallas_call(build_kernel, out_shape=(jax.ShapeDtypeStruct((TOEPLITZ_RO...  2.62 us
    pallas_call x1, Pallas kernels, spread(): pl.pallas_call(spread_kernel, out_shape=jax.ShapeDtypeStruct((segments, b...  1.71 us
  transfers between devices with their start and end apart: 1, of which 1 were waited for; matrix products, arithmetic and copies ran while one was open for 0% of the time, Pallas kernels for 5%

profile of v1, /device:TPU:0, one launch (start us, length us, event | category | flops | bytes accessed | tf_op | source)
XLA Modules:
  0.0 57.2 jit_solution(15996481973668875139)
XLA Ops:
  0.0 1.7 %spread_beams.1 = bf16[16,64,128]{2,1,0:T(8,128)(2,1)} custom-call(bf16[64,2048]{1,0:T(8,128)(2,1)} %signal_ref.1), custom_call_target="tpu_custom_call" | custom-call | tf_op jit(solution)/shard_map/spread_beams/pallas_call | solution.py:50
  1.7 7.4 %all-to-all-start = ((bf16[16,64,128]{2,1,0:T(8,128)(2,1)}), bf16[16,64,128]{2,1,0:T(8,128)(2,1)S(1)}, u32[]{:S(2)}, u32[]{:S(2)}) async-start(bf16[16,64,128]{2,1,0:T(8,128)(2,1)} %spread_beams.1), calls=%async_computation | async-start | bytes 524288 | tf_op jit(solution)/shard_map/all_to_all | solution.py:316
  9.1 0.0 copy-start
  9.1 0.8 %copy-done = f32[16384]{0:T(1024)S(1)} copy-done((f32[16384]{0:T(1024)S(1)}, f32[16384]{0:T(1024)}, u32[]{:S(2)}) %copy-start) | copy-done | bytes 65560
  9.9 0.0 copy-start.1
  10.0 0.7 %copy-done.1 = s32[2,128,8]{1,2,0:T(8,128)S(1)} copy-done((s32[2,128,8]{1,2,0:T(8,128)S(1)}, s32[2,128,8]{1,2,0:T(8,128)}, u32[]{:S(2)}) %copy-start.1) | copy-done | bytes 8216
  10.6 0.0 copy-start.2
  10.6 0.7 %copy-done.2 = f32[2,128,8]{1,2,0:T(8,128)S(1)} copy-done((f32[2,128,8]{1,2,0:T(8,128)S(1)}, f32[2,128,8]{1,2,0:T(8,128)}, u32[]{:S(2)}) %copy-start.2) | copy-done | bytes 8216
  11.3 2.6 %build_toeplitz.1 = (bf16[16768,128]{1,0:T(8,128)(2,1)S(1)}, bf16[256,256]{1,0:T(8,128)(2,1)S(1)}) custom-call(f32[128,128]{1,0:T(8,128)S(1)} %bitcast.5, s32[2,8,128]{2,1,0:T(8,128)S(1)} %bitcast.6, f32[2,8,128]{2,1,0:T(8,128)S(1)} %bitcast.7), custom_call_target="tpu_custom_call" | custom-call | flops 10000000 | bytes 16000000 | tf_op jit(solution)/shard_map/build_toeplitz/pallas_call | solution.py:97
  14.0 0.0 copy-start.3
  14.0 2.0 %copy-done.3 = bf16[16768,128]{1,0:T(8,128)(2,1)} copy-done((bf16[16768,128]{1,0:T(8,128)(2,1)}, bf16[16768,128]{1,0:T(8,128)(2,1)S(1)}, u32[]{:S(2)}) %copy-start.3) | copy-done | bytes 4292632
  15.9 3.2 %all-to-all-done = bf16[16,64,128]{2,1,0:T(8,128)(2,1)S(1)} async-done(((bf16[16,64,128]{2,1,0:T(8,128)(2,1)}), bf16[16,64,128]{2,1,0:T(8,128)(2,1)S(1)}, u32[]{:S(2)}, u32[]{:S(2)}) %all-to-all-start) | async-done | bytes 262176 | tf_op jit(solution)/shard_map/all_to_all | solution.py:316
  19.2 0.0 copy-start.4
  19.2 2.2 %copy-done.4 = bf16[16768,128]{1,0:T(8,128)(2,1)S(1)} copy-done((bf16[16768,128]{1,0:T(8,128)(2,1)S(1)}, bf16[16768,128]{1,0:T(8,128)(2,1)}, u32[]{:S(2)}) %copy-start.4) | copy-done | bytes 4292632
  21.4 0.0 copy-start.5
  21.4 0.7 %copy-done.5 = s32[2,256]{1,0:T(2,128)S(1)} copy-done((s32[2,256]{1,0:T(2,128)S(1)}, s32[2,256]{1,0:T(2,128)}, u32[]{:S(2)}) %copy-start.5) | copy-done | bytes 2072
  22.1 11.3 %warp_correlate.1 = bf16[16,144,128]{2,1,0:T(8,128)(2,1)S(1)} custom-call(s32[2,256]{1,0:T(2,128)S(1)} %copy-done.5, bf16[1024,128]{1,0:T(8,128)(2,1)S(1)} %bitcast.4, bf16[256,256]{1,0:T(8,128)(2,1)S(1)} %get-tuple-element.7.interp_ref, bf16[16768,128]{1,0:T(8,128)(2,1)S(1)} %copy-done.4), custom_call_target="tpu_custom_call" | custom-call | flops 8724152320 | bytes 12000000 | tf_op jit(solution)/shard_map/warp_correlate/pallas_call | solution.py:225
  33.3 20.5 %all_to_all.10.power_ref.sums_ref = bf16[16,144,128]{2,1,0:T(8,128)(2,1)} all-to-all(bf16[16,144,128]{2,1,0:T(8,128)(2,1)S(1)} %warp_correlate.1), channel_id=1, replica_groups=mesh['groups'=2,'tm'=16] {'tm'}, dimensions={0} | all-to-all | bytes 1179648 | tf_op jit(solution)/shard_map/all_to_all | solution.py:331
  53.9 3.3 %scale_power.1 = bf16[2,64,2048]{2,1,0:T(8,128)(2,1)} custom-call(bf16[16,144,128]{2,1,0:T(8,128)(2,1)} %all_to_all.10.power_ref.sums_ref, bf16[16,144,128]{2,1,0:T(8,128)(2,1)} %all_to_all.10.power_ref.sums_ref), custom_call_target="tpu_custom_call" | custom-call | flops 1000000 | bytes 1200000 | tf_op jit(solution)/shard_map/scale_power/pallas_call | solution.py:271
Async XLA Ops:
  1.7 17.4 %all-to-all-start = ((bf16[16,64,128]{2,1,0:T(8,128)(2,1)}), bf16[16,64,128]{2,1,0:T(8,128)(2,1)S(1)}, u32[]{:S(2)}, u32[]{:S(2)}) async-start(bf16[16,64,128]{2,1,0:T(8,128)(2,1)} %spread_beams.1), calls=%async_computation | async-start | bytes 524288 | tf_op jit(solution)/shard_map/all_to_all | solution.py:316
  9.1 0.8 %copy-start = (f32[16384]{0:T(1024)S(1)}, f32[16384]{0:T(1024)}, u32[]{:S(2)}) copy-start(f32[16384]{0:T(1024)} %param.9) | copy-start | bytes 196612
  9.9 0.7 %copy-start.1 = (s32[2,128,8]{1,2,0:T(8,128)S(1)}, s32[2,128,8]{1,2,0:T(8,128)}, u32[]{:S(2)}) copy-start(s32[2,128,8]{1,2,0:T(8,128)} %param.7) | copy-start | bytes 24580
  10.6 0.7 %copy-start.2 = (f32[2,128,8]{1,2,0:T(8,128)S(1)}, f32[2,128,8]{1,2,0:T(8,128)}, u32[]{:S(2)}) copy-start(f32[2,128,8]{1,2,0:T(8,128)} %param.8) | copy-start | bytes 24580
  14.0 2.0 %copy-start.3 = (bf16[16768,128]{1,0:T(8,128)(2,1)}, bf16[16768,128]{1,0:T(8,128)(2,1)S(1)}, u32[]{:S(2)}) copy-start(bf16[16768,128]{1,0:T(8,128)(2,1)S(1)} %get-tuple-element.8.strips_ref) | copy-start | bytes 12877828
  19.2 2.2 %copy-start.4 = (bf16[16768,128]{1,0:T(8,128)(2,1)S(1)}, bf16[16768,128]{1,0:T(8,128)(2,1)}, u32[]{:S(2)}) copy-start(bf16[16768,128]{1,0:T(8,128)(2,1)} %copy-done.3) | copy-start | bytes 12877828
  21.4 0.7 %copy-start.5 = (s32[2,256]{1,0:T(2,128)S(1)}, s32[2,256]{1,0:T(2,128)}, u32[]{:S(2)}) copy-start(s32[2,256]{1,0:T(2,128)} %sources_ref.1) | copy-start | bytes 6148
